TPU v7x, 32 devices: a whole 2x2x4 slice. The times are simulated.
32 devices in a mesh: parts: 2 (over y), rot: 4 (over z), batch: 2 (over x), wt: 2 (over core).
Axes of the slice: x: 2, y: 2, z: 4, core: 2. Of those that a mesh axis runs over, the one named last changes fastest.
Arguments:
- features: bfloat16 [4, 64, 8, 64, 256], P(('parts', 'batch'), 'rot', 'wt'), parts along dimension 0, may hold values from -6 to 6
- mix_weight: bfloat16 [3, 256, 256], replicated, may hold values from -0.21875 to 0.21875
- conv_weight: bfloat16 [9, 256, 256], replicated, may hold values from -0.125 to 0.125
- cotangent: bfloat16 [4, 64, 8, 64, 256], P(('parts', 'batch'), 'rot', 'wt'), parts along dimension 0, may hold values from -6 to 6
Outputs:
- output: bfloat16 [4, 64, 8, 64, 256], P(('parts', 'batch'), 'rot', 'wt'), parts along dimension 0
- grad_input: bfloat16 [4, 64, 8, 64, 256], P(('parts', 'batch'), 'rot', 'wt'), parts along dimension 0
- weight_grads: float32 [512, 12, 256], P(('parts', 'batch', 'wt'), None, 'rot'), parts along dimension 0
There are 2 independent parts, one for each index of `parts`. A program takes and returns all parts, laid end to end along the dimension named above; an argument that names none is the same for every part. Nothing has to cross between parts.
All inputs are finite; a program needn't handle non-finite values.
Results may differ from a plain program's by a relative error of at most 0.0055.
Values may be sent and summed in bfloat16 or wider, within the bound.
A program may use at most 128 MiB of HBM per device.

v0:
```python
import jax
import jax.numpy as jnp
from jax import lax
from jax.sharding import PartitionSpec as P


def with_halo(block, sides, width, periodic):
    for axis, dim in sides:
        count = lax.axis_size(axis)
        forward = [(i, i + 1) for i in range(count - 1)]
        if periodic:
            forward.append((count - 1, 0))
        backward = [(target, source) for source, target in forward]
        low = lax.ppermute(
            lax.slice_in_dim(block, block.shape[dim] - width, None, axis=dim), axis, forward
        )
        high = lax.ppermute(lax.slice_in_dim(block, 0, width, axis=dim), axis, backward)
        block = jnp.concatenate([low, block, high], axis=dim)
    return block


def contract_first(left, right):
    return lax.dot_general(
        left, right, (((0,), (0,)), ((), ())), preferred_element_type=jnp.float32
    )


def contract_last(left, right):
    return lax.dot_general(
        left, right, (((1,), (1,)), ((), ())), preferred_element_type=jnp.float32
    )


def local(features, mix_weight, conv_weight, cotangent):
    block_shape = features.shape
    members = block_shape[1]
    height = block_shape[2]
    breadth = block_shape[3]
    channels = block_shape[4]
    taps = mix_weight.shape[0]
    feat_cycle = with_halo(features, (("rot", 1),), 1, True)
    cycle_rows = [
        feat_cycle[:, offset : offset + members].reshape(-1, channels) for offset in range(taps)
    ]
    mixed = jnp.zeros((cycle_rows[0].shape[0], channels), jnp.float32)
    for offset in range(taps):
        mixed = mixed + jnp.dot(
            cycle_rows[offset], mix_weight[offset], preferred_element_type=jnp.float32
        )
    mixed = mixed.astype(jnp.bfloat16).reshape(block_shape)
    mixed_rows = with_halo(mixed, (("wt", 2),), 1, False)
    mixed_pad = jnp.pad(mixed_rows, ((0, 0), (0, 0), (0, 0), (1, 1), (0, 0)))
    shifted = [
        mixed_pad[:, :, row : row + height, col : col + breadth].reshape(-1, channels)
        for row in range(3)
        for col in range(3)
    ]
    active = jnp.zeros((cycle_rows[0].shape[0], channels), jnp.float32)
    for tap_index in range(9):
        active = active + jnp.dot(
            shifted[tap_index], conv_weight[tap_index], preferred_element_type=jnp.float32
        )
    sigma = jax.nn.sigmoid(active)
    feat_flat = features.reshape(-1, channels).astype(jnp.float32)
    output = (feat_flat + active * sigma).astype(jnp.bfloat16).reshape(block_shape)
    cot_flat = cotangent.reshape(-1, channels).astype(jnp.float32)
    slope = (cot_flat * (sigma * (1.0 + active * (1.0 - sigma)))).astype(jnp.bfloat16)
    slope_rows = with_halo(slope.reshape(block_shape), (("wt", 2),), 1, False)
    slope_pad = jnp.pad(slope_rows, ((0, 0), (0, 0), (0, 0), (1, 1), (0, 0)))
    back = jnp.zeros((cycle_rows[0].shape[0], channels), jnp.float32)
    for row in range(3):
        for col in range(3):
            piece = slope_pad[
                :, :, 2 - row : 2 - row + height, 2 - col : 2 - col + breadth
            ].reshape(-1, channels)
            back = back + contract_last(piece, conv_weight[3 * row + col])
    mixed_grad = back.astype(jnp.bfloat16)
    grad_cycle = with_halo(mixed_grad.reshape(block_shape), (("rot", 1),), 1, True)
    total = cot_flat
    for offset in range(taps):
        piece = grad_cycle[:, 2 - offset : 2 - offset + members].reshape(-1, channels)
        total = total + contract_last(piece, mix_weight[offset])
    grad_input = total.astype(jnp.bfloat16).reshape(block_shape)
    pieces = [contract_first(mixed_grad, cycle_rows[offset]) for offset in range(taps)]
    pieces = pieces + [contract_first(slope, shifted[tap_index]) for tap_index in range(9)]
    partial_grads = lax.psum_scatter(
        jnp.stack(pieces, axis=1), ("batch", "wt"), scatter_dimension=0, tiled=True
    )
    grads = lax.psum_scatter(partial_grads, "rot", scatter_dimension=2, tiled=True)
    return (output, grad_input, grads)


def solution(mesh):
    placed = (
        P(("parts", "batch"), "rot", "wt", None, None),
        P(),
        P(),
        P(("parts", "batch"), "rot", "wt", None, None),
    )
    return jax.shard_map(
        local,
        mesh=mesh,
        in_specs=placed,
        out_specs=(
            P(("parts", "batch"), "rot", "wt", None, None),
            P(("parts", "batch"), "rot", "wt", None, None),
            P(("parts", "batch", "wt"), None, "rot"),
        ),
        check_vma=False,
    )
```

profile of v0, /device:TPU:0, one launch (start us, length us, event | category | flops | bytes accessed | tf_op | source)
XLA Modules:
  0.0 171.9 jit_solution(14267449528913405065)
XLA Ops:
  8.2 3.1 %collective-permute-start = (bf16[1,1,4,64,256]{4,3,2,1,0:T(8,128)(2,1)S(1)}, bf16[1,1,4,64,256]{4,3,2,1,0:T(8,128)(2,1)S(1)}, u32[]{:S(2)}, u32[]{:S(2)}) collective-permute-start(bf16[1,1,4,64,256]{4,3,2,1,0:T(8,128)(2,1)S(1)} %get-tuple-element.31), channel_id=1, source_target_pairs={{0,4},{4,8},{8,12},{12,0},{1,5},{5,9},{9,13},{13,1},{2,6},{6,10},{... | collective-permute-start | bytes 393224 | tf_op jit(solution)/shard_map/ppermute | solution.py:14
  11.3 2.1 %collective-permute-start.1 = (bf16[1,1,4,64,256]{4,3,2,1,0:T(8,128)(2,1)S(1)}, bf16[1,1,4,64,256]{4,3,2,1,0:T(8,128)(2,1)S(1)}, u32[]{:S(2)}, u32[]{:S(2)}) collective-permute-start(bf16[1,1,4,64,256]{4,3,2,1,0:T(8,128)(2,1)S(1)} %get-tuple-element.32), channel_id=1, source_target_pairs={{4,0},{8,4},{12,8},{0,12},{5,1},{9,5},{13,9},{1,13},{6,2},{10,6},{... | collective-permute-start | bytes 393224 | tf_op jit(solution)/shard_map/ppermute | solution.py:17
  13.4 2.4 %fusion.49 = f32[4096,256]{1,0:T(8,128)S(1)} fusion(bf16[4096,256]{1,0:T(8,128)(2,1)} %bitcast.199, bf16[3,256,256]{2,1,0:T(8,128)(2,1)} %param.5), kind=kOutput, calls=%fused_computation.95 | convolution fusion | flops 536870912 | bytes 6422528 | tf_op jit(solution)/shard_map/dot_general | solution.py:47
  15.8 1.8 %collective-permute-done = bf16[1,1,4,64,256]{4,3,2,1,0:T(8,128)(2,1)S(1)} collective-permute-done((bf16[1,1,4,64,256]{4,3,2,1,0:T(8,128)(2,1)S(1)}, bf16[1,1,4,64,256]{4,3,2,1,0:T(8,128)(2,1)S(1)}, u32[]{:S(2)}, u32[]{:S(2)}) %collective-permute-start) | collective-permute-done | bytes 131104 | tf_op jit(solution)/shard_map/ppermute | solution.py:14
  24.0 2.3 %collective-permute-done.3 = bf16[1,16,1,64,256]{4,3,2,1,0:T(8,128)(2,1)S(1)} collective-permute-done((bf16[1,16,1,64,256]{4,3,2,1,0:T(8,128)(2,1)S(1)}, bf16[1,16,1,64,256]{4,3,2,1,0:T(8,128)(2,1)S(1)}, u32[]{:S(2)}, u32[]{:S(2)}) %collective-permute-start.3) | collective-permute-done | bytes 524320 | tf_op jit(solution)/shard_map/ppermute | solution.py:17
  26.3 1.8 %select_maximum_fusion.2 = bf16[1,16,6,66,256]{4,3,2,1,0:T(8,128)(2,1)S(1)} fusion(bf16[1,16,1,64,256]{4,3,2,1,0:T(8,128)(2,1)S(1)} %collective-permute-done.3, bf16[1,16,4,64,256]{4,3,2,1,0:T(8,128)(2,1)S(1)} %bitcast.192, bf16[1,16,1,64,256]{4,3,2,1,0:T(8,128)(2,1)S(1)} %collective-permute-done.2), kind=kLoop, calls=%fused_computation.33 | loop fusion | flops 19464192 | bytes 6389760 | tf_op jit(solution)/shard_map/concatenate | solution.py:18
  28.1 4.8 %fusion.78 = (bf16[1,16,4,64,256]{4,3,2,1,0:T(8,128)(2,1)S(1)}, bf16[1,16,4,64,256]{4,3,2,1,0:T(8,128)(2,1)S(1)}, bf16[1,16,4,64,256]{4,3,2,1,0:T(8,128)(2,1)S(1...) fusion(bf16[1,16,6,66,256]{4,3,2,1,0:T(8,128)(2,1)S(1)} %select, ...), kind=kLoop, calls=%fused_computation.124 | loop fusion | bytes 25165824 | tf_op jit(solution)/shard_map/slice | solution.py:54
  33.6 2.1 %pad_maximum_fusion.4 = (bf16[1,16,4,64,256]{4,3,2,1,0:T(8,128)(2,1)}, bf16[1,16,4,64,256]{4,3,2,1,0:T(8,128)(2,1)S(1)}) fusion(bf16[1,16,1,64,256]{4,3,2,1,0:T(8,128)(2,1)S(1)} %collective-permute-done.3, bf16[1,16,4,64,256]{4,3,2,1,0:T(8,128)(2,1)S(1)} %bitcast.193, bf16[1,16,1,64,256]{4,3,2,1,0:T(8,128)(2,1)S(1)} %collective-permute-done.2), kind=kLoop, calls=%fused_computation.40 | loop fusion | flops 2097152 | bytes 7340032 | tf_op jit(solution)/shard_map/concatenate | solution.py:18
  43.1 4.1 %fusion.8 = (bf16[4096,256]{1,0:T(8,128)(2,1)S(1)}, bf16[4096,256]{1,0:T(8,128)(2,1)}) fusion(bf16[1,16,4,64,256]{4,3,2,1,0:T(8,128)(2,1)S(1)} %copy-done.17, bf16[1,16,4,64,256]{4,3,2,1,0:T(8,128)(2,1)S(1)} %copy-done, f32[4096,256]{1,0:T(8,128)S(1)} %fusion.24, f32[4096,256]{1,0:T(8,128)S(1)} %convolution_add_fusion.10, ...), kind=kOutput, calls=%fused_computation.28 | convolution fusion | flops 553648128 | bytes 19005440 | tf_op jit(solution)/shard_map/dot_general | solution.py:60
  47.3 2.1 %collective-permute-start.4 = (bf16[1,16,1,64,256]{4,3,2,1,0:T(8,128)(2,1)S(1)}, bf16[1,16,1,64,256]{4,3,2,1,0:T(8,128)(2,1)S(1)}, u32[]{:S(2)}, u32[]{:S(2)}) collective-permute-start(bf16[1,16,1,64,256]{4,3,2,1,0:T(8,128)(2,1)S(1)} %get-tuple-element.23), channel_id=1, source_target_pairs={{0,1},{2,3},{4,5},{6,7},{8,9},{10,11},{12,13},{14,15},{16,17},{18,... | collective-permute-start | bytes 1572872 | tf_op jit(solution)/shard_map/ppermute | solution.py:14
  50.9 2.3 %collective-permute-done.5 = bf16[1,16,1,64,256]{4,3,2,1,0:T(8,128)(2,1)S(1)} collective-permute-done((bf16[1,16,1,64,256]{4,3,2,1,0:T(8,128)(2,1)S(1)}, bf16[1,16,1,64,256]{4,3,2,1,0:T(8,128)(2,1)S(1)}, u32[]{:S(2)}, u32[]{:S(2)}) %collective-permute-start.5) | collective-permute-done | bytes 524320 | tf_op jit(solution)/shard_map/ppermute | solution.py:17
  53.9 1.8 %select_maximum_fusion = bf16[1,16,6,66,256]{4,3,2,1,0:T(8,128)(2,1)S(1)} fusion(bf16[1,16,1,64,256]{4,3,2,1,0:T(8,128)(2,1)S(1)} %collective-permute-done.5, bf16[1,16,4,64,256]{4,3,2,1,0:T(8,128)(2,1)S(1)} %bitcast.197, bf16[1,16,1,64,256]{4,3,2,1,0:T(8,128)(2,1)S(1)} %collective-permute-done.4), kind=kLoop, calls=%fused_computation.31 | loop fusion | flops 19464192 | bytes 6389760 | tf_op jit(solution)/shard_map/concatenate | solution.py:18
  55.7 6.2 %fusion.77 = (bf16[1,16,4,64,256]{4,3,2,1,0:T(8,128)(2,1)S(1)}, bf16[1,16,4,64,256]{4,3,2,1,0:T(8,128)(2,1)S(1)}, bf16[1,16,4,64,256]{4,3,2,1,0:T(8,128)(2,1)}, ...) fusion(bf16[1,16,6,66,256]{4,3,2,1,0:T(8,128)(2,1)S(1)} %select, ...), kind=kLoop, calls=%fused_computation.123 | loop fusion | bytes 25165824 | tf_op jit(solution)/shard_map/slice | solution.py:73
  61.9 1.7 %fusion.40 = f32[4096,256]{1,0:T(8,128)S(1)} fusion(bf16[4096,256]{1,0:T(8,128)(2,1)S(1)} %bitcast.208, bf16[9,256,256]{2,1,0:T(8,128)(2,1)} %param.6), kind=kOutput, calls=%fused_computation.86 | convolution fusion | flops 536870912 | bytes 6422528 | tf_op jit(solution)/shard_map/dot_general | solution.py:29
  65.3 2.5 %convolution_add_fusion.8 = f32[4096,256]{1,0:T(8,128)S(1)} fusion(f32[4096,256]{1,0:T(8,128)S(1)} %fusion.40, bf16[4096,256]{1,0:T(8,128)(2,1)} %bitcast.228, bf16[9,256,256]{2,1,0:T(8,128)(2,1)S(1)} %copy-done.12), kind=kOutput, calls=%fused_computation.13 | convolution fusion | flops 537919488 | bytes 10616832 | tf_op jit(solution)/shard_map/dot_general | solution.py:29
  75.1 1.8 %fusion.7 = bf16[4096,256]{1,0:T(8,128)(2,1)S(1)} fusion(f32[4096,256]{1,0:T(8,128)S(1)} %fusion.22, f32[4096,256]{1,0:T(8,128)S(1)} %convolution_add_fusion.3, bf16[4096,256]{1,0:T(8,128)(2,1)S(1)} %bitcast.211, bf16[9,256,256]{2,1,0:T(8,128)(2,1)} %param.6), kind=kOutput, calls=%fused_computation.27 | convolution fusion | flops 540016640 | bytes 12713984 | tf_op jit(solution)/shard_map/dot_general | solution.py:29
  90.5 1.7 %fusion.12 = f32[256,12,256]{2,0,1:T(8,128)} fusion(f32[256,12,256]{2,0,1:T(8,128)} %fusion.13, bf16[4096,256]{1,0:T(8,128)(2,1)S(1)} %get-tuple-element.3, bf16[4096,256]{1,0:T(8,128)(2,1)S(1)} %bitcast.214), kind=kOutput, calls=%fused_computation.49 | convolution fusion | flops 536870912 | bytes 4456448 | tf_op jit(solution)/shard_map/dot_general | solution.py:23
  95.2 1.8 %collective-permute-start.7 = (bf16[1,1,4,64,256]{4,3,2,1,0:T(8,128)(2,1)S(1)}, bf16[1,1,4,64,256]{4,3,2,1,0:T(8,128)(2,1)S(1)}, u32[]{:S(2)}, u32[]{:S(2)}) collective-permute-start(bf16[1,1,4,64,256]{4,3,2,1,0:T(8,128)(2,1)S(1)} %get-tuple-element.19), channel_id=1, source_target_pairs={{0,4},{4,8},{8,12},{12,0},{1,5},{5,9},{9,13},{13,1},{2,6},{6,10},{... | collective-permute-start | bytes 393224 | tf_op jit(solution)/shard_map/ppermute | solution.py:14
  97.1 2.1 %collective-permute-start.6 = (bf16[1,1,4,64,256]{4,3,2,1,0:T(8,128)(2,1)S(1)}, bf16[1,1,4,64,256]{4,3,2,1,0:T(8,128)(2,1)S(1)}, u32[]{:S(2)}, u32[]{:S(2)}) collective-permute-start(bf16[1,1,4,64,256]{4,3,2,1,0:T(8,128)(2,1)S(1)} %get-tuple-element.20), channel_id=1, source_target_pairs={{4,0},{8,4},{12,8},{0,12},{5,1},{9,5},{13,9},{1,13},{6,2},{10,6},{... | collective-permute-start | bytes 393224 | tf_op jit(solution)/shard_map/ppermute | solution.py:17
  99.1 34.1 %reduce-scatter.5.cloned.1.call-done = f32[64,12,256]{2,0,1:T(8,128)} async-done(((f32[256,12,256]{2,0,1:T(8,128)}), f32[64,12,256]{2,0,1:T(8,128)}) %reduce-scatter.5.cloned.1.call-update) | async-done | bytes 786448 | tf_op jit(solution)/shard_map/reduce_scatter | solution.py:86
  133.2 3.6 %copy.7 = f32[64,12,256]{0,1,2:T(8,128)} copy(f32[64,12,256]{2,0,1:T(8,128)} %reduce-scatter.5.cloned.1.call-done) | data formatting | bytes 1572864
  136.8 2.8 %reshape.119 = f32[256,768]{1,0:T(8,128)} reshape(f32[256,12,64]{2,1,0:T(8,128)} %bitcast.229) | data formatting | bytes 1572864
  142.7 2.1 %fusion.5 = bf16[4096,256]{1,0:T(8,128)(2,1)} fusion(f32[4096,256]{1,0:T(8,128)S(1)} %fusion.1, bf16[4096,256]{1,0:T(8,128)(2,1)S(1)} %bitcast.227, bf16[3,256,256]{2,1,0:T(8,128)(2,1)S(1)} %copy-done.22), kind=kOutput, calls=%fused_computation.25 | convolution fusion | flops 538968064 | bytes 8519680 | tf_op jit(solution)/shard_map/dot_general | solution.py:29
  144.8 18.3 %reduce-scatter.7.cloned.1.call-done = f32[64,768]{1,0:T(8,128)} async-done(((f32[256,768]{1,0:T(8,128)}), f32[64,768]{1,0:T(8,128)}) %reduce-scatter.7.cloned.1.call-update) | async-done | bytes 196624
  (96 shorter events, 48.2 us)
Async XLA Ops:
  7.2 126.0 %reduce-scatter.5.cloned.1.call-start = ((), (), s32[]{:S(2)}) async-start(), calls=%async_computation.2 | async-start | bytes 3932160 | tf_op jit(solution)/shard_map/reduce_scatter | solution.py:86
  8.2 9.4 %collective-permute-start = (bf16[1,1,4,64,256]{4,3,2,1,0:T(8,128)(2,1)S(1)}, bf16[1,1,4,64,256]{4,3,2,1,0:T(8,128)(2,1)S(1)}, u32[]{:S(2)}, u32[]{:S(2)}) collective-permute-start(bf16[1,1,4,64,256]{4,3,2,1,0:T(8,128)(2,1)S(1)} %get-tuple-element.31), channel_id=1, source_target_pairs={{0,4},{4,8},{8,12},{12,0},{1,5},{5,9},{9,13},{13,1},{2,6},{6,10},{... | collective-permute-start | bytes 393224 | tf_op jit(solution)/shard_map/ppermute | solution.py:14
  11.3 7.8 %collective-permute-start.1 = (bf16[1,1,4,64,256]{4,3,2,1,0:T(8,128)(2,1)S(1)}, bf16[1,1,4,64,256]{4,3,2,1,0:T(8,128)(2,1)S(1)}, u32[]{:S(2)}, u32[]{:S(2)}) collective-permute-start(bf16[1,1,4,64,256]{4,3,2,1,0:T(8,128)(2,1)S(1)} %get-tuple-element.32), channel_id=1, source_target_pairs={{4,0},{8,4},{12,8},{0,12},{5,1},{9,5},{13,9},{1,13},{6,2},{10,6},{... | collective-permute-start | bytes 393224 | tf_op jit(solution)/shard_map/ppermute | solution.py:17
  13.4 5.7 %copy-start = (bf16[1,16,4,64,256]{4,3,2,1,0:T(8,128)(2,1)S(1)}, bf16[1,16,4,64,256]{4,3,2,1,0:T(8,128)(2,1)}, u32[]{:S(2)}) copy-start(bf16[1,16,4,64,256]{4,3,2,1,0:T(8,128)(2,1)} %param.4) | copy-start | bytes 6291460
  15.8 3.6 %copy-start.21 = (bf16[3,256,256]{2,1,0:T(8,128)(2,1)S(1)}, bf16[3,256,256]{2,1,0:T(8,128)(2,1)}, u32[]{:S(2)}) copy-start(bf16[3,256,256]{2,1,0:T(8,128)(2,1)} %param.5) | copy-start | bytes 1179652
  21.1 2.8 %collective-permute-start.2 = (bf16[1,16,1,64,256]{4,3,2,1,0:T(8,128)(2,1)S(1)}, bf16[1,16,1,64,256]{4,3,2,1,0:T(8,128)(2,1)S(1)}, u32[]{:S(2)}, u32[]{:S(2)}) collective-permute-start(bf16[1,16,1,64,256]{4,3,2,1,0:T(8,128)(2,1)S(1)} %get-tuple-element.27), channel_id=1, source_target_pairs={{0,1},{2,3},{4,5},{6,7},{8,9},{10,11},{12,13},{14,15},{16,17},{18,... | collective-permute-start | bytes 1572872 | tf_op jit(solution)/shard_map/ppermute | solution.py:14
  22.5 3.8 %collective-permute-start.3 = (bf16[1,16,1,64,256]{4,3,2,1,0:T(8,128)(2,1)S(1)}, bf16[1,16,1,64,256]{4,3,2,1,0:T(8,128)(2,1)S(1)}, u32[]{:S(2)}, u32[]{:S(2)}) collective-permute-start(bf16[1,16,1,64,256]{4,3,2,1,0:T(8,128)(2,1)S(1)} %get-tuple-element.28), channel_id=1, source_target_pairs={{1,0},{3,2},{5,4},{7,6},{9,8},{11,10},{13,12},{15,14},{17,16},{19,... | collective-permute-start | bytes 1572872 | tf_op jit(solution)/shard_map/ppermute | solution.py:17
  28.1 4.9 %copy-start.11 = (bf16[9,256,256]{2,1,0:T(8,128)(2,1)S(1)}, bf16[9,256,256]{2,1,0:T(8,128)(2,1)}, u32[]{:S(2)}) copy-start(bf16[9,256,256]{2,1,0:T(8,128)(2,1)} %param.6) | copy-start | bytes 3538948
  32.9 4.1 %copy-start.5 = (bf16[1,16,4,64,256]{4,3,2,1,0:T(8,128)(2,1)}, bf16[1,16,4,64,256]{4,3,2,1,0:T(8,128)(2,1)S(1)}, u32[]{:S(2)}) copy-start(bf16[1,16,4,64,256]{4,3,2,1,0:T(8,128)(2,1)S(1)} %get-tuple-element.14) | copy-start | bytes 6291460
  32.9 4.9 %copy-start.3 = (bf16[1,16,4,64,256]{4,3,2,1,0:T(8,128)(2,1)}, bf16[1,16,4,64,256]{4,3,2,1,0:T(8,128)(2,1)S(1)}, u32[]{:S(2)}) copy-start(bf16[1,16,4,64,256]{4,3,2,1,0:T(8,128)(2,1)S(1)} %get-tuple-element.13) | copy-start | bytes 6291460
  32.9 7.1 %copy-start.1 = (bf16[1,16,4,64,256]{4,3,2,1,0:T(8,128)(2,1)}, bf16[1,16,4,64,256]{4,3,2,1,0:T(8,128)(2,1)S(1)}, u32[]{:S(2)}) copy-start(bf16[1,16,4,64,256]{4,3,2,1,0:T(8,128)(2,1)S(1)} %get-tuple-element.12) | copy-start | bytes 6291460
  40.9 2.2 %copy-start.19 = (bf16[1,16,4,64,256]{4,3,2,1,0:T(8,128)(2,1)S(1)}, bf16[1,16,4,64,256]{4,3,2,1,0:T(8,128)(2,1)}, u32[]{:S(2)}) copy-start(bf16[1,16,4,64,256]{4,3,2,1,0:T(8,128)(2,1)} %get-tuple-element.25) | copy-start | bytes 6291460
  47.3 3.6 %collective-permute-start.4 = (bf16[1,16,1,64,256]{4,3,2,1,0:T(8,128)(2,1)S(1)}, bf16[1,16,1,64,256]{4,3,2,1,0:T(8,128)(2,1)S(1)}, u32[]{:S(2)}, u32[]{:S(2)}) collective-permute-start(bf16[1,16,1,64,256]{4,3,2,1,0:T(8,128)(2,1)S(1)} %get-tuple-element.23), channel_id=1, source_target_pairs={{0,1},{2,3},{4,5},{6,7},{8,9},{10,11},{12,13},{14,15},{16,17},{18,... | collective-permute-start | bytes 1572872 | tf_op jit(solution)/shard_map/ppermute | solution.py:14
  49.3 3.8 %collective-permute-start.5 = (bf16[1,16,1,64,256]{4,3,2,1,0:T(8,128)(2,1)S(1)}, bf16[1,16,1,64,256]{4,3,2,1,0:T(8,128)(2,1)S(1)}, u32[]{:S(2)}, u32[]{:S(2)}) collective-permute-start(bf16[1,16,1,64,256]{4,3,2,1,0:T(8,128)(2,1)S(1)} %get-tuple-element.24), channel_id=1, source_target_pairs={{1,0},{3,2},{5,4},{7,6},{9,8},{11,10},{13,12},{15,14},{17,16},{19,... | collective-permute-start | bytes 1572872 | tf_op jit(solution)/shard_map/ppermute | solution.py:17
  50.9 2.3 %copy-start.13 = (bf16[1,16,1,64,256]{4,3,2,1,0:T(8,128)(2,1)}, bf16[1,16,1,64,256]{4,3,2,1,0:T(8,128)(2,1)S(1)}, u32[]{:S(2)}) copy-start(bf16[1,16,1,64,256]{4,3,2,1,0:T(8,128)(2,1)S(1)} %collective-permute-done.4) | copy-start | bytes 1572868
  61.9 1.7 %copy-start.14 = (bf16[1,16,1,64,256]{4,3,2,1,0:T(8,128)(2,1)S(1)}, bf16[1,16,1,64,256]{4,3,2,1,0:T(8,128)(2,1)}, u32[]{:S(2)}) copy-start(bf16[1,16,1,64,256]{4,3,2,1,0:T(8,128)(2,1)} %copy-done.13) | copy-start | bytes 1572868
  61.9 1.7 %copy-start.16 = (bf16[1,16,1,64,256]{4,3,2,1,0:T(8,128)(2,1)S(1)}, bf16[1,16,1,64,256]{4,3,2,1,0:T(8,128)(2,1)}, u32[]{:S(2)}) copy-start(bf16[1,16,1,64,256]{4,3,2,1,0:T(8,128)(2,1)} %copy-done.15) | copy-start | bytes 1572868
  63.7 1.6 copy-start.12
  65.3 2.5 %copy-start.10 = (bf16[1,16,4,64,256]{4,3,2,1,0:T(8,128)(2,1)S(1)}, bf16[1,16,4,64,256]{4,3,2,1,0:T(8,128)(2,1)}, u32[]{:S(2)}) copy-start(bf16[1,16,4,64,256]{4,3,2,1,0:T(8,128)(2,1)} %get-tuple-element.8) | copy-start | bytes 6291460
  90.5 1.7 %copy-start.20 = (bf16[1,16,4,64,256]{4,3,2,1,0:T(8,128)(2,1)S(1)}, bf16[1,16,4,64,256]{4,3,2,1,0:T(8,128)(2,1)}, u32[]{:S(2)}) copy-start(bf16[1,16,4,64,256]{4,3,2,1,0:T(8,128)(2,1)} %get-tuple-element.25) | copy-start | bytes 6291460
  95.2 67.9 %reduce-scatter.7.cloned.1.call-start = ((), (), s32[]{:S(2)}) async-start(), calls=%async_computation.3 | async-start | bytes 983040
  95.2 45.1 %collective-permute-start.7 = (bf16[1,1,4,64,256]{4,3,2,1,0:T(8,128)(2,1)S(1)}, bf16[1,1,4,64,256]{4,3,2,1,0:T(8,128)(2,1)S(1)}, u32[]{:S(2)}, u32[]{:S(2)}) collective-permute-start(bf16[1,1,4,64,256]{4,3,2,1,0:T(8,128)(2,1)S(1)} %get-tuple-element.19), channel_id=1, source_target_pairs={{0,4},{4,8},{8,12},{12,0},{1,5},{5,9},{9,13},{13,1},{2,6},{6,10},{... | collective-permute-start | bytes 393224 | tf_op jit(solution)/shard_map/ppermute | solution.py:14
  97.1 43.3 %collective-permute-start.6 = (bf16[1,1,4,64,256]{4,3,2,1,0:T(8,128)(2,1)S(1)}, bf16[1,1,4,64,256]{4,3,2,1,0:T(8,128)(2,1)S(1)}, u32[]{:S(2)}, u32[]{:S(2)}) collective-permute-start(bf16[1,1,4,64,256]{4,3,2,1,0:T(8,128)(2,1)S(1)} %get-tuple-element.20), channel_id=1, source_target_pairs={{4,0},{8,4},{12,8},{0,12},{5,1},{9,5},{13,9},{1,13},{6,2},{10,6},{... | collective-permute-start | bytes 393224 | tf_op jit(solution)/shard_map/ppermute | solution.py:17
  136.8 2.8 %copy-start.22 = (bf16[3,256,256]{2,1,0:T(8,128)(2,1)S(1)}, bf16[3,256,256]{2,1,0:T(8,128)(2,1)}, u32[]{:S(2)}) copy-start(bf16[3,256,256]{2,1,0:T(8,128)(2,1)} %param.5) | copy-start | bytes 1179652
  (9 other events, 13.3 us)
Sparse Core Ops, SparseCore 0:
  95.3 37.8 reduce-scatter.4
  139.7 23.3 reduce-scatter.6
where the time goes:
time: 172 us
  waiting for transfers between devices  60.2 us (35%)
  matrix products  47.8 us (28%)
  local copies, waits for them, and re-layouts  25.9 us (15%)
  starting transfers between devices  15.5 us (9%)
  between operations  14.5 us (8%)
  other arithmetic  8 us (5%)
    reduce_scatter x1, waiting for transfers between devices, local(): lax.psum_scatter(jnp.stack(pieces, axis=1), ('batch', 'wt'), scatter_dime...  34.1 us
    unnamed x3, waiting for transfers between devices  18.3 us
    dot_general x12, matrix products, contract_first(): lax.dot_general(left, right, (((0,), (0,)), ((), ())), preferred_element_...  17.7 us
    dot_general x12, matrix products, contract_last(): lax.dot_general(left, right, (((1,), (1,)), ((), ())), preferred_element_...  16 us
    unnamed x50, local copies, waits for them, and re-layouts  13.7 us
    dot_general x9, matrix products, local(): jnp.dot(shifted[tap_index], conv_weight[tap_index], preferred_element_typ...  10.1 us
    ppermute x4, starting transfers between devices, with_halo(): lax.ppermute(lax.slice_in_dim(block, block.shape[dim] - width, None, axis...  8.29 us
    concatenate x6, other arithmetic, with_halo(): block = jnp.concatenate([low, block, high], axis=dim)  8 us
  transfers between devices with their start and end apart: 10, of which 6 were waited for; matrix products, arithmetic and copies ran while one was open for 7% of the time, Pallas kernels for 0%

commit v1 on v0

v1 whole, which is shorter than its diff:
```python
import functools

import jax
import jax.numpy as jnp
from jax import lax
from jax.experimental import pallas as pl
from jax.experimental.pallas import tpu as pltpu
from jax.sharding import PartitionSpec as P

MESH = pl.DeviceIdType.MESH
F32 = jnp.float32
BF16 = jnp.bfloat16


def dot(left, right):
    return jnp.dot(left, right, preferred_element_type=F32)


def join_rows(pieces):
    return jnp.concatenate(pieces, axis=0)


def join_lanes(pieces):
    return jnp.concatenate(pieces, axis=1)


def kernel(
    cfg, feat_hbm, mixw_hbm, convw_hbm, cot_hbm, out_ref, gin_ref, wgm_ref, wgc_ref,
    feat, cot, wmix, wconv, wmix_t, wconv_t, mbuf, sbuf, slope_t, mgrad_t, mgrad,
    mix_send, mix_recv, slope_send, slope_recv,
    acc_m, acc_c, s1m, s1c, r1m, r1c, s2m, s2c, r2m, r2c, o2m, o2c, s3m, s3c, r3m, r3c, o3m, o3c,
    load_sem, halo_sem, row_sem, sem1, sem2, sem3,
):
    n, height, breadth, ch, nrot, nbatch = cfg
    size = height * breadth
    chunk = ch // (nbatch * 2)
    width = ch // nrot
    rot = lax.axis_index("rot")
    bat = lax.axis_index("batch")
    wt = lax.axis_index("wt")
    other = 1 - wt
    right, left = lax.rem(rot + 1, nrot), lax.rem(rot + nrot - 1, nrot)

    def load(k, src, dst):
        copy = pltpu.make_async_copy(src, dst, load_sem.at[k])
        copy.start()
        return copy

    load_feat = load(0, feat_hbm, feat.at[pl.ds(size, n * size)])
    load_mix = load(1, mixw_hbm, wmix)
    load_conv = load(2, convw_hbm, wconv)
    load_cot = load(3, cot_hbm, cot)

    barrier = pltpu.get_barrier_semaphore()
    pl.semaphore_signal(barrier, inc=1, device_id={"wt": other}, device_id_type=MESH)
    for d in range(1, nbatch):
        pl.semaphore_signal(
            barrier, inc=1, device_id={"batch": lax.rem(bat + d, nbatch)}, device_id_type=MESH
        )
    for d in range(1, nrot):
        pl.semaphore_signal(
            barrier, inc=1, device_id={"rot": lax.rem(rot + d, nrot)}, device_id_type=MESH
        )
    pl.semaphore_wait(barrier, nbatch + nrot - 1)

    def remote(src, dst, send, recv, axis, index):
        copy = pltpu.make_async_remote_copy(
            src_ref=src, dst_ref=dst, send_sem=send, recv_sem=recv,
            device_id={axis: index}, device_id_type=MESH,
        )
        copy.start()
        return copy

    feat_left = remote(
        feat_hbm.at[pl.ds(0, size)], feat.at[pl.ds((n + 1) * size, size)],
        halo_sem.at[0], halo_sem.at[1], "rot", left,
    )
    feat_right = remote(
        feat_hbm.at[pl.ds((n - 1) * size, size)], feat.at[pl.ds(0, size)],
        halo_sem.at[2], halo_sem.at[3], "rot", right,
    )

    def column(rows):
        return lax.rem(lax.broadcasted_iota(jnp.int32, (rows, ch), 0), breadth)

    def spread(value):
        rows = value.shape[0]
        col = column(rows)
        before = jnp.where(col == 0, 0.0, pltpu.roll(value, 1, 0))
        after = jnp.where(col == breadth - 1, 0.0, pltpu.roll(value, rows - 1, 0))
        return join_lanes([before.astype(BF16), value.astype(BF16), after.astype(BF16)])

    def slot(g):
        return g - 1

    def place(g, at, value, buf, edge_buf):
        buf[g, pl.ds(breadth, size), :] = spread(value)
        low = value[size - breadth :]
        high = value[:breadth]
        edge_buf[at] = jnp.where(wt == 0, low, high).astype(BF16)

    near = (1 - wt) * (height + 1) * breadth
    far = wt * (height + 1) * breadth

    def place_halo(g, at, buf, recv):
        buf[g, pl.ds(pl.multiple_of(near, breadth), breadth), :] = spread(recv[at].astype(F32))
        buf[g, pl.ds(pl.multiple_of(far, breadth), breadth), :] = jnp.zeros((breadth, 3 * ch), BF16)

    def rows_of(g):
        return pl.ds(pl.multiple_of(g * size, size), size)

    def cycle(buf, g):
        return join_lanes([buf[rows_of(g + t), :] for t in range(3)])

    def window(buf, g):
        return join_lanes([buf[g, pl.ds(i * breadth, size), :] for i in range(3)])

    def mix_pair(gs, slots):
        value = dot(join_rows([cycle(feat, g) for g in gs]), wmix[...])
        for k, (g, at) in enumerate(zip(gs, slots)):
            place(g, at, value[k * size : (k + 1) * size], mbuf, mix_send)

    def active_pair(gs, slots):
        value = dot(join_rows([window(mbuf, g) for g in gs]), wconv[...])
        for k, (g, at) in enumerate(zip(gs, slots)):
            active = value[k * size : (k + 1) * size]
            sigma = 0.5 * jnp.tanh(0.5 * active) + 0.5
            out_ref[rows_of(g), :] = (
                feat[rows_of(g + 1), :].astype(F32) + active * sigma
            ).astype(BF16)
            slope = cot[rows_of(g), :].astype(F32) * (sigma * (1.0 + active * (1.0 - sigma)))
            place(g, at, slope, sbuf, slope_send)
            slope_t[g] = slope.astype(BF16).T

    def conv_grad_pair(gs):
        lhs = join_lanes([slope_t[g] for g in gs])
        for i in range(3):
            rhs = join_rows([mbuf[g, pl.ds(i * breadth, size), :] for g in gs])
            acc_c[:, pl.ds(i * 3 * ch, 3 * ch)] += dot(lhs, rhs)

    def back_pair(gs):
        value = dot(join_rows([window(sbuf, g) for g in gs]), wconv_t[...]).astype(BF16)
        for k, g in enumerate(gs):
            part = value[k * size : (k + 1) * size]
            mgrad[rows_of(g + 1), :] = part
            mgrad_t[g] = part.T

    def mix_grad_pair(gs):
        lhs = join_lanes([mgrad_t[g] for g in gs])
        for t in range(3):
            rhs = join_rows([feat[rows_of(g + t), :] for g in gs])
            acc_m[:, pl.ds(t * ch, ch)] += dot(lhs, rhs)

    def input_pair(gs):
        value = dot(join_rows([cycle(mgrad, g) for g in gs]), wmix_t[...])
        for k, g in enumerate(gs):
            gin_ref[rows_of(g), :] = (
                cot[rows_of(g), :].astype(F32) + value[k * size : (k + 1) * size]
            ).astype(BF16)

    edges = (0, n - 1)
    edge_slots = (n - 2, n - 1)

    def interior(body):
        def step(k, carry):
            g = 2 * k + 1
            body(g)
            return carry

        lax.fori_loop(0, (n - 2) // 2, step, 0)

    def start_rows(k, send, recv, edge):
        where = pl.ds(n - 2, 2) if edge else pl.ds(0, n - 2)
        return remote(
            send.at[where], recv.at[where], row_sem.at[2 * k], row_sem.at[2 * k + 1], "wt", other
        )

    def start_first(acc, s1, r1, k):
        for b in range(nbatch):
            start = pl.multiple_of((2 * b + other) * chunk, chunk)
            s1[pl.ds(b * chunk, chunk), :] = acc[pl.ds(start, chunk), :].astype(BF16)
        return remote(s1, r1, sem1.at[2 * k], sem1.at[2 * k + 1], "wt", other)

    def total_first(acc, r1, b):
        start = pl.multiple_of((2 * b + wt) * chunk, chunk)
        place_in = pl.multiple_of(b * chunk, chunk)
        return acc[pl.ds(start, chunk), :] + r1[pl.ds(place_in, chunk), :].astype(F32)

    def start_second(first, acc, r1, s2, r2, o2, k):
        first.wait()
        copies = []
        for d in range(1, nbatch):
            b = lax.rem(bat + d, nbatch)
            s2[d - 1] = total_first(acc, r1, b).astype(BF16)
            copies.append(
                remote(
                    s2.at[d - 1], r2.at[d - 1],
                    sem2.at[k, 2 * d - 2], sem2.at[k, 2 * d - 1], "batch", b,
                )
            )
        o2[...] = total_first(acc, r1, bat)
        return copies

    def start_third(second, o2, r2, s3, r3, o3, k, taps):
        for copy in second:
            copy.wait()
        total = o2[...]
        for d in range(1, nbatch):
            total = total + r2[d - 1].astype(F32)
        for q in range(nrot):
            piece = join_lanes(
                [total[:, t * ch + q * width : t * ch + (q + 1) * width] for t in range(taps)]
            )
            o3[q] = piece
            s3[q] = piece.astype(BF16)
        copies = []
        for d in range(1, nrot):
            q = lax.rem(rot + d, nrot)
            copies.append(
                remote(
                    s3.at[q], r3.at[d - 1], sem3.at[k, 2 * d - 2], sem3.at[k, 2 * d - 1], "rot", q
                )
            )
        return copies

    def finish(third, o3, r3, result):
        for copy in third:
            copy.wait()
        total = o3[rot]
        for d in range(1, nrot):
            total = total + r3[d - 1].astype(F32)
        result[...] = total

    load_mix.wait()
    load_feat.wait()
    interior(lambda g: mix_pair((g, g + 1), (slot(g), slot(g + 1))))
    mix_in = start_rows(0, mix_send, mix_recv, False)

    for k in range(3):
        wmix_t[pl.ds(k * ch, ch), :] = wmix[pl.ds((2 - k) * ch, ch), :].T
    load_conv.wait()
    for k in range(9):
        wconv_t[pl.ds(k * ch, ch), :] = wconv[pl.ds((8 - k) * ch, ch), :].T
    acc_c[...] = jnp.zeros_like(acc_c)
    acc_m[...] = jnp.zeros_like(acc_m)
    load_cot.wait()

    mix_in.wait()

    def forward(g):
        for k in range(2):
            place_halo(g + k, slot(g + k), mbuf, mix_recv)
        active_pair((g, g + 1), (slot(g), slot(g + 1)))

    interior(forward)
    slope_in = start_rows(1, slope_send, slope_recv, False)

    feat_left.wait()
    feat_right.wait()
    mix_pair(edges, edge_slots)
    mix_edge = start_rows(2, mix_send, mix_recv, True)
    interior(lambda g: conv_grad_pair((g, g + 1)))
    mix_edge.wait()
    for g, at in zip(edges, edge_slots):
        place_halo(g, at, mbuf, mix_recv)
    active_pair(edges, edge_slots)
    slope_edge = start_rows(3, slope_send, slope_recv, True)
    conv_grad_pair(edges)
    first_c = start_first(acc_c, s1c, r1c, 0)

    slope_edge.wait()
    for g, at in zip(edges, edge_slots):
        place_halo(g, at, sbuf, slope_recv)
    back_pair(edges)
    grad_left = remote(
        mgrad.at[pl.ds(size, size)], mgrad.at[pl.ds((n + 1) * size, size)],
        halo_sem.at[4], halo_sem.at[5], "rot", left,
    )
    grad_right = remote(
        mgrad.at[pl.ds(n * size, size)], mgrad.at[pl.ds(0, size)],
        halo_sem.at[6], halo_sem.at[7], "rot", right,
    )
    second_c = start_second(first_c, acc_c, r1c, s2c, r2c, o2c, 0)
    slope_in.wait()

    def backward(g):
        for k in range(2):
            place_halo(g + k, slot(g + k), sbuf, slope_recv)
        back_pair((g, g + 1))

    interior(backward)

    def mix_grads(k, carry):
        mix_grad_pair((2 * k, 2 * k + 1))
        return carry

    lax.fori_loop(0, n // 2, mix_grads, 0)
    first_m = start_first(acc_m, s1m, r1m, 1)
    third_c = start_third(second_c, o2c, r2c, s3c, r3c, o3c, 0, 9)
    second_m = start_second(first_m, acc_m, r1m, s2m, r2m, o2m, 1)
    interior(lambda g: input_pair((g, g + 1)))
    third_m = start_third(second_m, o2m, r2m, s3m, r3m, o3m, 1, 3)
    grad_left.wait()
    grad_right.wait()
    input_pair(edges)
    finish(third_c, o3c, r3c, wgc_ref)
    finish(third_m, o3m, r3m, wgm_ref)


def local(cfg, features, mix_weight, conv_weight, cotangent):
    n, height, breadth, ch, nrot, nbatch = cfg
    size = height * breadth
    chunk = ch // (nbatch * 2)
    width = ch // nrot
    rows = n * size
    shape = jax.ShapeDtypeStruct
    vmem = pltpu.VMEM

    def stages(make):
        return [make(3), make(9)]

    scratch = [
        vmem((rows + 2 * size, ch), BF16),
        vmem((rows, ch), BF16),
        vmem((3 * ch, ch), BF16),
        vmem((9 * ch, ch), BF16),
        vmem((3 * ch, ch), BF16),
        vmem((9 * ch, ch), BF16),
        vmem((n, size + 2 * breadth, 3 * ch), BF16),
        vmem((n, size + 2 * breadth, 3 * ch), BF16),
        vmem((n, ch, size), BF16),
        vmem((n, ch, size), BF16),
        vmem((rows + 2 * size, ch), BF16),
    ]
    scratch += [vmem((n, breadth, ch), BF16) for _ in range(4)]
    scratch += stages(lambda t: vmem((ch, t * ch), F32))
    scratch += stages(lambda t: vmem((nbatch * chunk, t * ch), BF16))
    scratch += stages(lambda t: vmem((nbatch * chunk, t * ch), BF16))
    scratch += stages(lambda t: vmem((nbatch - 1, chunk, t * ch), BF16))
    scratch += stages(lambda t: vmem((nbatch - 1, chunk, t * ch), BF16))
    scratch += stages(lambda t: vmem((chunk, t * ch), F32))
    scratch += stages(lambda t: vmem((nrot, chunk, t * width), BF16))
    scratch += stages(lambda t: vmem((nrot - 1, chunk, t * width), BF16))
    scratch += stages(lambda t: vmem((nrot, chunk, t * width), F32))
    dma = pltpu.SemaphoreType.DMA
    scratch += [
        dma((4,)), dma((8,)), dma((8,)), dma((4,)),
        dma((2, 2 * (nbatch - 1))), dma((2, 2 * (nrot - 1))),
    ]
    whole = pl.BlockSpec(memory_space=pltpu.VMEM)
    output, grad_input, grads_mix, grads_conv = pl.pallas_call(
        functools.partial(kernel, cfg),
        out_shape=(
            shape((rows, ch), BF16),
            shape((rows, ch), BF16),
            shape((chunk, 3 * width), F32),
            shape((chunk, 9 * width), F32),
        ),
        in_specs=[pl.BlockSpec(memory_space=pl.ANY)] * 4,
        out_specs=(whole, whole, whole, whole),
        scratch_shapes=scratch,
        compiler_params=pltpu.CompilerParams(
            collective_id=0, has_side_effects=True, vmem_limit_bytes=60 * 2**20
        ),
    )(
        features.reshape(rows, ch),
        mix_weight.reshape(3 * ch, ch),
        conv_weight.reshape(9 * ch, ch),
        cotangent.reshape(rows, ch),
    )
    grads = jnp.concatenate(
        [grads_mix.reshape(chunk, 3, width), grads_conv.reshape(chunk, 9, width)], axis=1
    )
    return output.reshape(features.shape), grad_input.reshape(features.shape), grads


def solution(mesh):
    spec = P(("parts", "batch"), "rot", "wt", None, None)

    def run(features, mix_weight, conv_weight, cotangent):
        nrot, nbatch = mesh.shape["rot"], mesh.shape["batch"]
        cfg = (
            features.shape[1] // nrot,
            features.shape[2] // mesh.shape["wt"],
            features.shape[3],
            features.shape[4],
            nrot,
            nbatch,
        )
        return jax.shard_map(
            functools.partial(local, cfg),
            mesh=mesh,
            in_specs=(spec, P(), P(), spec),
            out_specs=(spec, spec, P(("parts", "batch", "wt"), None, "rot")),
            check_vma=False,
        )(features, mix_weight, conv_weight, cotangent)

    return run
```

time: 172 us -> 57.7 us (0.34)
  waiting for transfers between devices: 60.2 us -> 0 us
  Pallas kernels: 0 us -> 50 us
  matrix products: 47.8 us -> 0 us
  local copies, waits for them, and re-layouts: 25.9 us -> 6.73 us
  starting transfers between devices: 15.5 us -> 0 us
  between operations: 14.5 us -> 0.66 us
  other arithmetic: 8 us -> 0.03 us
    pallas_call x0 -> x1, Pallas kernels: none -> 50 us  [local(): pl.pallas_call(functools.partial(kernel, cfg), out_shape=(shape((rows, ch...]
    dot_general x36 -> x0, matrix products: 47.8 us -> none  [the longest x12 17.7 us: contract_first(): lax.dot_general(left, right, (((0,), (0,)), ((), ())), preferred_element_...]
    reduce_scatter x1 -> x0, waiting for transfers between devices: 34.1 us -> none  [local(): lax.psum_scatter(jnp.stack(pieces, axis=1), ('batch', 'wt'), scatter_dime...]
    unnamed x3 -> x0, waiting for transfers between devices: 18.3 us -> none
    ppermute x8 -> x0, starting transfers between devices: 15.4 us -> none  [the longest x4 8.29 us: with_halo(): lax.ppermute(lax.slice_in_dim(block, block.shape[dim] - width, None, axis...]
    slice x6 -> x0, local copies, waits for them, and re-layouts: 12.2 us -> none  [the longest x1 6.2 us: local(): slope_pad[:, :, 2 - row:2 - row + height, 2 - col:2 - col + breadth]]
    unnamed x50 -> x7, local copies, waits for them, and re-layouts: 13.7 us -> 4.58 us
    concatenate x6 -> x1, other arithmetic: 8 us -> 0.03 us  [local(): jnp.concatenate([grads_mix.reshape(chunk, 3, width), grads_conv.reshape(c...]
  transfers between devices with their start and end apart: 10 -> 0, of which waited for: 6 -> 0; matrix products, arithmetic and copies ran while one was open for 7% -> 0% of each run, Pallas kernels for 0% -> 0%
where the time goes in v1:
time: 57.7 us; the launch traced here: 57.5 us
  Pallas kernels  50 us (87%)
  local copies, waits for them, and re-layouts  6.73 us (12%)
  between operations  0.66 us (1%)
    pallas_call x1, Pallas kernels, local(): pl.pallas_call(functools.partial(kernel, cfg), out_shape=(shape((rows, ch...  50 us
    unnamed x7, local copies, waits for them, and re-layouts  4.58 us
    pallas_call x2, local copies, waits for them, and re-layouts, local(): pl.pallas_call(functools.partial(kernel, cfg), out_shape=(shape((rows, ch...  2.15 us

profile of v1, /device:TPU:0, one launch (start us, length us, event | category | flops | bytes accessed | tf_op | source)
XLA Modules:
  0.0 57.5 jit_solution(220841922082182548)
XLA Ops:
  0.6 50.0 %shard_map.67 = (bf16[4096,256]{1,0:T(8,128)(2,1)}, bf16[4096,256]{1,0:T(8,128)(2,1)}, f32[64,192]{1,0:T(8,128)}, f32[64,576]{1,0:T(8,128)}) custom-call(bf16[4096,256]{1,0:T(8,128)(2,1)} %bitcast.10, bf16[768,256]{1,0:T(8,128)(2,1)} %bitcast.14, bf16[2304,256]{1,0:T(8,128)(2,1)} %bitcast.13, bf16[4096,256]{1,0:T(8,128)(2,1)} %bitcast.11), custom_call_target="tpu_custom_call" | custom-call | tf_op jit(solution)/shard_map/pallas_call | solution.py:351
  50.7 0.0 copy-start.1
  50.7 1.1 %copy.9 = f32[64,192]{0,1:T(8,128)S(1)} copy(f32[64,192]{1,0:T(8,128)} %get-tuple-element.9) | data formatting | bytes 98304 | tf_op jit(solution)/shard_map/pallas_call | solution.py:351
  51.8 1.1 %copy.10 = f32[64,576]{0,1:T(8,128)S(1)} copy(f32[64,576]{1,0:T(8,128)} %get-tuple-element.10) | data formatting | bytes 294912 | tf_op jit(solution)/shard_map/pallas_call | solution.py:351
  52.9 0.9 %copy.11 = f32[64,12,64]{2,0,1:T(8,128)} copy(f32[64,12,64]{0,2,1:T(8,128)S(1)} %pad_maximum_fusion) | data formatting | bytes 393216
  53.8 0.0 copy-done.1
  53.8 0.0 copy-start
  53.8 1.3 %copy.14 = bf16[1,16,4,64,256]{4,3,2,1,0:T(8,128)(2,1)} copy(bf16[1,16,4,64,256]{4,3,2,1,0:T(8,128)(2,1)S(1)} %bitcast.9) | data formatting | bytes 4194304
  55.1 1.0 %copy-done = bf16[4096,256]{1,0:T(8,128)(2,1)S(1)} copy-done((bf16[4096,256]{1,0:T(8,128)(2,1)S(1)}, bf16[4096,256]{1,0:T(8,128)(2,1)}, u32[]{:S(2)}) %copy-start) | copy-done | bytes 2097176
  56.1 1.3 %copy.15 = bf16[1,16,4,64,256]{4,3,2,1,0:T(8,128)(2,1)} copy(bf16[1,16,4,64,256]{4,3,2,1,0:T(8,128)(2,1)S(1)} %bitcast.8) | data formatting | bytes 4194304
  (1 shorter events, 0.0 us)
Async XLA Ops:
  50.7 3.1 %copy-start.1 = (bf16[4096,256]{1,0:T(8,128)(2,1)S(1)}, bf16[4096,256]{1,0:T(8,128)(2,1)}, u32[]{:S(2)}) copy-start(bf16[4096,256]{1,0:T(8,128)(2,1)} %get-tuple-element.7) | copy-start | bytes 6291460
  53.8 2.3 %copy-start = (bf16[4096,256]{1,0:T(8,128)(2,1)S(1)}, bf16[4096,256]{1,0:T(8,128)(2,1)}, u32[]{:S(2)}) copy-start(bf16[4096,256]{1,0:T(8,128)(2,1)} %get-tuple-element.8) | copy-start | bytes 6291460

commit v2 on v1

--- a/solution.py
+++ b/solution.py
@@ -25,11 +25,11 @@
 
 
 def kernel(
-    cfg, feat_hbm, mixw_hbm, convw_hbm, cot_hbm, out_ref, gin_ref, wgm_ref, wgc_ref,
-    feat, cot, wmix, wconv, wmix_t, wconv_t, mbuf, sbuf, slope_t, mgrad_t, mgrad,
+    cfg, feat_hbm, mixw_hbm, convw_hbm, cot_hbm, out_hbm, gin_hbm, grads_ref,
+    out_ref, gin_ref, feat, cot, wmix, wconv, wmix_t, wconv_t, mbuf, sbuf, slope_t, mgrad_t, mgrad,
     mix_send, mix_recv, slope_send, slope_recv,
     acc_m, acc_c, s1m, s1c, r1m, r1c, s2m, s2c, r2m, r2c, o2m, o2c, s3m, s3c, r3m, r3c, o3m, o3c,
-    load_sem, halo_sem, row_sem, sem1, sem2, sem3,
+    load_sem, store_sem, halo_sem, row_sem, sem1, sem2, sem3,
 ):
     n, height, breadth, ch, nrot, nbatch = cfg
     size = height * breadth
@@ -43,6 +43,12 @@
 
     def load(k, src, dst):
         copy = pltpu.make_async_copy(src, dst, load_sem.at[k])
+        copy.start()
+        return copy
+
+    def store(k, src, dst, start, count):
+        where = pl.ds(start * size, count * size)
+        copy = pltpu.make_async_copy(src.at[where], dst.at[where], store_sem.at[k])
         copy.start()
         return copy
 
@@ -106,6 +112,10 @@
         buf[g, pl.ds(pl.multiple_of(near, breadth), breadth), :] = spread(recv[at].astype(F32))
         buf[g, pl.ds(pl.multiple_of(far, breadth), breadth), :] = jnp.zeros((breadth, 3 * ch), BF16)
 
+    def place_halos(g, buf, recv):
+        for k in range(2):
+            place_halo(g + k, slot(g + k), buf, recv)
+
     def rows_of(g):
         return pl.ds(pl.multiple_of(g * size, size), size)
 
@@ -115,13 +125,17 @@
     def window(buf, g):
         return join_lanes([buf[g, pl.ds(i * breadth, size), :] for i in range(3)])
 
-    def mix_pair(gs, slots):
-        value = dot(join_rows([cycle(feat, g) for g in gs]), wmix[...])
+    def mix_product(gs):
+        return dot(join_rows([cycle(feat, g) for g in gs]), wmix[...])
+
+    def mix_after(gs, slots, value):
         for k, (g, at) in enumerate(zip(gs, slots)):
             place(g, at, value[k * size : (k + 1) * size], mbuf, mix_send)
 
-    def active_pair(gs, slots):
-        value = dot(join_rows([window(mbuf, g) for g in gs]), wconv[...])
+    def active_product(gs):
+        return dot(join_rows([window(mbuf, g) for g in gs]), wconv[...])
+
+    def active_after(gs, slots, value):
         for k, (g, at) in enumerate(zip(gs, slots)):
             active = value[k * size : (k + 1) * size]
             sigma = 0.5 * jnp.tanh(0.5 * active) + 0.5
@@ -138,8 +152,11 @@
             rhs = join_rows([mbuf[g, pl.ds(i * breadth, size), :] for g in gs])
             acc_c[:, pl.ds(i * 3 * ch, 3 * ch)] += dot(lhs, rhs)
 
-    def back_pair(gs):
-        value = dot(join_rows([window(sbuf, g) for g in gs]), wconv_t[...]).astype(BF16)
+    def back_product(gs):
+        return dot(join_rows([window(sbuf, g) for g in gs]), wconv_t[...])
+
+    def back_after(gs, slots, value):
+        value = value.astype(BF16)
         for k, g in enumerate(gs):
             part = value[k * size : (k + 1) * size]
             mgrad[rows_of(g + 1), :] = part
@@ -151,8 +168,10 @@
             rhs = join_rows([feat[rows_of(g + t), :] for g in gs])
             acc_m[:, pl.ds(t * ch, ch)] += dot(lhs, rhs)
 
-    def input_pair(gs):
-        value = dot(join_rows([cycle(mgrad, g) for g in gs]), wmix_t[...])
+    def input_product(gs):
+        return dot(join_rows([cycle(mgrad, g) for g in gs]), wmix_t[...])
+
+    def input_after(gs, slots, value):
         for k, g in enumerate(gs):
             gin_ref[rows_of(g), :] = (
                 cot[rows_of(g), :].astype(F32) + value[k * size : (k + 1) * size]
@@ -168,6 +187,27 @@
             return carry
 
         lax.fori_loop(0, (n - 2) // 2, step, 0)
+
+    def at_ends(product, after):
+        after(edges, edge_slots, product(edges))
+
+    pairs = (n - 2) // 2
+    third_part = pairs // 3
+
+    def staggered(product, after, begin=0, end=pairs):
+        if begin == end:
+            return
+
+        def step(k, value):
+            g = 2 * k + 1
+            following = product((g, g + 1))
+            after((g - 2, g - 1), (g - 3, g - 2), value)
+            return following
+
+        first = 2 * begin + 1
+        value = lax.fori_loop(begin + 1, end, step, product((first, first + 1)))
+        last = 2 * end - 1
+        after((last, last + 1), (last - 1, last), value)
 
     def start_rows(k, send, recv, edge):
         where = pl.ds(n - 2, 2) if edge else pl.ds(0, n - 2)
@@ -223,17 +263,18 @@
             )
         return copies
 
-    def finish(third, o3, r3, result):
+    def finish(third, o3, r3, base, taps):
         for copy in third:
             copy.wait()
         total = o3[rot]
         for d in range(1, nrot):
             total = total + r3[d - 1].astype(F32)
-        result[...] = total
+        for t in range(taps):
+            grads_ref[base + t] = total[:, t * width : (t + 1) * width]
 
     load_mix.wait()
     load_feat.wait()
-    interior(lambda g: mix_pair((g, g + 1), (slot(g), slot(g + 1))))
+    staggered(mix_product, mix_after)
     mix_in = start_rows(0, mix_send, mix_recv, False)
 
     for k in range(3):
@@ -247,31 +288,32 @@
 
     mix_in.wait()
 
-    def forward(g):
-        for k in range(2):
-            place_halo(g + k, slot(g + k), mbuf, mix_recv)
-        active_pair((g, g + 1), (slot(g), slot(g + 1)))
-
-    interior(forward)
+    interior(lambda g: place_halos(g, mbuf, mix_recv))
+    staggered(active_product, active_after)
     slope_in = start_rows(1, slope_send, slope_recv, False)
 
     feat_left.wait()
     feat_right.wait()
-    mix_pair(edges, edge_slots)
+    at_ends(mix_product, mix_after)
     mix_edge = start_rows(2, mix_send, mix_recv, True)
     interior(lambda g: conv_grad_pair((g, g + 1)))
     mix_edge.wait()
     for g, at in zip(edges, edge_slots):
         place_halo(g, at, mbuf, mix_recv)
-    active_pair(edges, edge_slots)
+    at_ends(active_product, active_after)
+    store_out = store(0, out_ref, out_hbm, 0, n)
     slope_edge = start_rows(3, slope_send, slope_recv, True)
     conv_grad_pair(edges)
     first_c = start_first(acc_c, s1c, r1c, 0)
 
+    slope_in.wait()
+    interior(lambda g: place_halos(g, sbuf, slope_recv))
+    staggered(back_product, back_after, 0, third_part)
+    second_c = start_second(first_c, acc_c, r1c, s2c, r2c, o2c, 0)
     slope_edge.wait()
     for g, at in zip(edges, edge_slots):
         place_halo(g, at, sbuf, slope_recv)
-    back_pair(edges)
+    at_ends(back_product, back_after)
     grad_left = remote(
         mgrad.at[pl.ds(size, size)], mgrad.at[pl.ds((n + 1) * size, size)],
         halo_sem.at[4], halo_sem.at[5], "rot", left,
@@ -280,31 +322,32 @@
         mgrad.at[pl.ds(n * size, size)], mgrad.at[pl.ds(0, size)],
         halo_sem.at[6], halo_sem.at[7], "rot", right,
     )
-    second_c = start_second(first_c, acc_c, r1c, s2c, r2c, o2c, 0)
-    slope_in.wait()
-
-    def backward(g):
-        for k in range(2):
-            place_halo(g + k, slot(g + k), sbuf, slope_recv)
-        back_pair((g, g + 1))
-
-    interior(backward)
+    staggered(back_product, back_after, third_part, pairs)
 
     def mix_grads(k, carry):
         mix_grad_pair((2 * k, 2 * k + 1))
         return carry
 
+    third_c = start_third(second_c, o2c, r2c, s3c, r3c, o3c, 0, 9)
     lax.fori_loop(0, n // 2, mix_grads, 0)
     first_m = start_first(acc_m, s1m, r1m, 1)
-    third_c = start_third(second_c, o2c, r2c, s3c, r3c, o3c, 0, 9)
+    staggered(input_product, input_after, 0, 2 * third_part)
     second_m = start_second(first_m, acc_m, r1m, s2m, r2m, o2m, 1)
-    interior(lambda g: input_pair((g, g + 1)))
-    third_m = start_third(second_m, o2m, r2m, s3m, r3m, o3m, 1, 3)
+    staggered(input_product, input_after, 2 * third_part, pairs)
+    store_in = store(1, gin_ref, gin_hbm, 1, n - 2)
     grad_left.wait()
     grad_right.wait()
-    input_pair(edges)
-    finish(third_c, o3c, r3c, wgc_ref)
-    finish(third_m, o3m, r3m, wgm_ref)
+    at_ends(input_product, input_after)
+    store_ends = [
+        store(2, gin_ref, gin_hbm, 0, 1), store(3, gin_ref, gin_hbm, n - 1, 1)
+    ]
+    third_m = start_third(second_m, o2m, r2m, s3m, r3m, o3m, 1, 3)
+    finish(third_c, o3c, r3c, 3, 9)
+    store_out.wait()
+    store_in.wait()
+    for copy in store_ends:
+        copy.wait()
+    finish(third_m, o3m, r3m, 0, 3)
 
 
 def local(cfg, features, mix_weight, conv_weight, cotangent):
@@ -320,6 +363,8 @@
         return [make(3), make(9)]
 
     scratch = [
+        vmem((rows, ch), BF16),
+        vmem((rows, ch), BF16),
         vmem((rows + 2 * size, ch), BF16),
         vmem((rows, ch), BF16),
         vmem((3 * ch, ch), BF16),
@@ -344,20 +389,20 @@
     scratch += stages(lambda t: vmem((nrot, chunk, t * width), F32))
     dma = pltpu.SemaphoreType.DMA
     scratch += [
-        dma((4,)), dma((8,)), dma((8,)), dma((4,)),
+        dma((4,)), dma((4,)), dma((8,)), dma((8,)), dma((4,)),
         dma((2, 2 * (nbatch - 1))), dma((2, 2 * (nrot - 1))),
     ]
+    remain = pl.BlockSpec(memory_space=pl.ANY)
     whole = pl.BlockSpec(memory_space=pltpu.VMEM)
-    output, grad_input, grads_mix, grads_conv = pl.pallas_call(
+    output, grad_input, grads = pl.pallas_call(
         functools.partial(kernel, cfg),
         out_shape=(
             shape((rows, ch), BF16),
             shape((rows, ch), BF16),
-            shape((chunk, 3 * width), F32),
-            shape((chunk, 9 * width), F32),
+            shape((12, chunk, width), F32),
         ),
-        in_specs=[pl.BlockSpec(memory_space=pl.ANY)] * 4,
-        out_specs=(whole, whole, whole, whole),
+        in_specs=[remain] * 4,
+        out_specs=(remain, remain, whole),
         scratch_shapes=scratch,
         compiler_params=pltpu.CompilerParams(
             collective_id=0, has_side_effects=True, vmem_limit_bytes=60 * 2**20
@@ -368,9 +413,7 @@
         conv_weight.reshape(9 * ch, ch),
         cotangent.reshape(rows, ch),
     )
-    grads = jnp.concatenate(
-        [grads_mix.reshape(chunk, 3, width), grads_conv.reshape(chunk, 9, width)], axis=1
-    )
+    grads = jnp.transpose(grads, (1, 0, 2))
     return output.reshape(features.shape), grad_input.reshape(features.shape), grads
 
 

time: 57.7 us -> 56.9 us (0.986)
  local copies, waits for them, and re-layouts: 6.73 us -> 5.38 us
  Pallas kernels: 50 us -> 50.7 us
    pallas_call x2 -> x0, local copies, waits for them, and re-layouts: 2.15 us -> none  [local(): pl.pallas_call(functools.partial(kernel, cfg), out_shape=(shape((rows, ch...]
    unnamed x7, local copies, waits for them, and re-layouts: 4.58 us -> 5.38 us
    pallas_call x1, Pallas kernels: 50 us -> 50.7 us  [local(): pl.pallas_call(functools.partial(kernel, cfg), out_shape=(shape((rows, ch...]
where the time goes in v2:
time: 56.9 us; the launch traced here: 56.8 us
  Pallas kernels  50.7 us (89%)
  local copies, waits for them, and re-layouts  5.38 us (9%)
  between operations  0.65 us (1%)
    pallas_call x1, Pallas kernels, local(): pl.pallas_call(functools.partial(kernel, cfg), out_shape=(shape((rows, ch...  50.7 us
    unnamed x7, local copies, waits for them, and re-layouts  5.38 us

profile of v2, /device:TPU:0, one launch (start us, length us, event | category | flops | bytes accessed | tf_op | source)
XLA Modules:
  0.0 56.8 jit_solution(353660444024813681)
XLA Ops:
  0.6 50.7 %shard_map.67 = (bf16[4096,256]{1,0:T(8,128)(2,1)}, bf16[4096,256]{1,0:T(8,128)(2,1)}, f32[12,64,64]{2,1,0:T(8,128)}) custom-call(bf16[4096,256]{1,0:T(8,128)(2,1)} %bitcast.9, bf16[768,256]{1,0:T(8,128)(2,1)} %bitcast.12, bf16[2304,256]{1,0:T(8,128)(2,1)} %bitcast.11, bf16[4096,256]{1,0:T(8,128)(2,1)} %bitcast.10), custom_call_target="tpu_custom_call" | custom-call | tf_op jit(solution)/shard_map/pallas_call | solution.py:397
  51.4 0.0 copy-start
  51.4 3.3 %copy.10 = bf16[1,16,4,64,256]{4,3,2,1,0:T(8,128)(2,1)} copy(bf16[1,16,4,64,256]{4,3,2,1,0:T(8,128)(2,1)} %bitcast.8) | data formatting | bytes 4194304
  54.7 0.0 copy-done
  54.7 0.0 copy-start.1
  54.7 1.3 %copy.11 = bf16[1,16,4,64,256]{4,3,2,1,0:T(8,128)(2,1)} copy(bf16[1,16,4,64,256]{4,3,2,1,0:T(8,128)(2,1)S(1)} %bitcast.7) | data formatting | bytes 4194304
  56.0 0.0 copy-done.1
  56.0 0.7 %copy.12 = f32[64,12,64]{2,0,1:T(8,128)} copy(f32[64,12,64]{2,0,1:T(8,128)S(1)} %bitcast.13) | data formatting | bytes 393216
Async XLA Ops:
  51.4 3.3 %copy-start = (bf16[4096,256]{1,0:T(8,128)(2,1)S(1)}, bf16[4096,256]{1,0:T(8,128)(2,1)}, u32[]{:S(2)}) copy-start(bf16[4096,256]{1,0:T(8,128)(2,1)} %get-tuple-element.7) | copy-start | bytes 6291460
  54.7 1.3 %copy-start.1 = (f32[12,64,64]{2,1,0:T(8,128)S(1)}, f32[12,64,64]{2,1,0:T(8,128)}, u32[]{:S(2)}) copy-start(f32[12,64,64]{2,1,0:T(8,128)} %get-tuple-element.8) | copy-start | bytes 589828

commit v3 on v2

--- a/solution.py
+++ b/solution.py
@@ -194,20 +194,16 @@
     pairs = (n - 2) // 2
     third_part = pairs // 3
 
-    def staggered(product, after, begin=0, end=pairs):
+    def inner_pairs(product, after, begin=0, end=pairs):
         if begin == end:
             return
 
-        def step(k, value):
+        def step(k, carry):
             g = 2 * k + 1
-            following = product((g, g + 1))
-            after((g - 2, g - 1), (g - 3, g - 2), value)
-            return following
-
-        first = 2 * begin + 1
-        value = lax.fori_loop(begin + 1, end, step, product((first, first + 1)))
-        last = 2 * end - 1
-        after((last, last + 1), (last - 1, last), value)
+            after((g, g + 1), (slot(g), slot(g + 1)), product((g, g + 1)))
+            return carry
+
+        lax.fori_loop(begin, end, step, 0)
 
     def start_rows(k, send, recv, edge):
         where = pl.ds(n - 2, 2) if edge else pl.ds(0, n - 2)
@@ -274,7 +270,7 @@
 
     load_mix.wait()
     load_feat.wait()
-    staggered(mix_product, mix_after)
+    inner_pairs(mix_product, mix_after)
     mix_in = start_rows(0, mix_send, mix_recv, False)
 
     for k in range(3):
@@ -289,7 +285,7 @@
     mix_in.wait()
 
     interior(lambda g: place_halos(g, mbuf, mix_recv))
-    staggered(active_product, active_after)
+    inner_pairs(active_product, active_after)
     slope_in = start_rows(1, slope_send, slope_recv, False)
 
     feat_left.wait()
@@ -308,7 +304,7 @@
 
     slope_in.wait()
     interior(lambda g: place_halos(g, sbuf, slope_recv))
-    staggered(back_product, back_after, 0, third_part)
+    inner_pairs(back_product, back_after, 0, third_part)
     second_c = start_second(first_c, acc_c, r1c, s2c, r2c, o2c, 0)
     slope_edge.wait()
     for g, at in zip(edges, edge_slots):
@@ -322,7 +318,7 @@
         mgrad.at[pl.ds(n * size, size)], mgrad.at[pl.ds(0, size)],
         halo_sem.at[6], halo_sem.at[7], "rot", right,
     )
-    staggered(back_product, back_after, third_part, pairs)
+    inner_pairs(back_product, back_after, third_part, pairs)
 
     def mix_grads(k, carry):
         mix_grad_pair((2 * k, 2 * k + 1))
@@ -331,9 +327,9 @@
     third_c = start_third(second_c, o2c, r2c, s3c, r3c, o3c, 0, 9)
     lax.fori_loop(0, n // 2, mix_grads, 0)
     first_m = start_first(acc_m, s1m, r1m, 1)
-    staggered(input_product, input_after, 0, 2 * third_part)
+    inner_pairs(input_product, input_after, 0, 2 * third_part)
     second_m = start_second(first_m, acc_m, r1m, s2m, r2m, o2m, 1)
-    staggered(input_product, input_after, 2 * third_part, pairs)
+    inner_pairs(input_product, input_after, 2 * third_part, pairs)
     store_in = store(1, gin_ref, gin_hbm, 1, n - 2)
     grad_left.wait()
     grad_right.wait()
@@ -348,6 +344,12 @@
     for copy in store_ends:
         copy.wait()
     finish(third_m, o3m, r3m, 0, 3)
+
+
+def hand_on(*refs):
+    count = len(refs) // 2
+    for source, target in zip(refs[:count], refs[count:]):
+        target[...] = source[...]
 
 
 def local(cfg, features, mix_weight, conv_weight, cotangent):
@@ -413,6 +415,22 @@
         conv_weight.reshape(9 * ch, ch),
         cotangent.reshape(rows, ch),
     )
+    steps = 4
+    tile = pl.BlockSpec((rows // steps, ch), lambda i: (i, 0))
+    full = pl.BlockSpec((12, chunk, width), lambda i: (0, 0, 0))
+    output, grad_input, grads = pl.pallas_call(
+        hand_on,
+        grid=(steps,),
+        out_shape=(
+            shape((rows, ch), BF16),
+            shape((rows, ch), BF16),
+            shape((12, chunk, width), F32),
+        ),
+        in_specs=[tile, tile, full],
+        out_specs=(tile, tile, full),
+        compiler_params=pltpu.CompilerParams(vmem_limit_bytes=24 * 2**20),
+        cost_estimate=pl.CostEstimate(flops=0, bytes_accessed=8 * rows * ch, transcendentals=0),
+    )(output, grad_input, grads)
     grads = jnp.transpose(grads, (1, 0, 2))
     return output.reshape(features.shape), grad_input.reshape(features.shape), grads
 

time: 56.9 us -> 57.8 us (1.016)
  Pallas kernels: 50.7 us -> 52.8 us
  local copies, waits for them, and re-layouts: 5.38 us -> 4.17 us
    pallas_call x0 -> x1, Pallas kernels: none -> 2.59 us  [local(): pl.pallas_call(hand_on, grid=(steps,), out_shape=(shape((rows, ch), BF16)...]
    unnamed x7 -> x6, local copies, waits for them, and re-layouts: 5.38 us -> 4.17 us
where the time goes in v3:
time: 57.8 us; the launch traced here: 57.6 us
  Pallas kernels  52.8 us (91%)
  local copies, waits for them, and re-layouts  4.17 us (7%)
  between operations  0.65 us (1%)
    pallas_call x1, Pallas kernels, local(): pl.pallas_call(functools.partial(kernel, cfg), out_shape=(shape((rows, ch...  50.2 us
    unnamed x6, local copies, waits for them, and re-layouts  4.17 us
    pallas_call x1, Pallas kernels, local(): pl.pallas_call(hand_on, grid=(steps,), out_shape=(shape((rows, ch), BF16)...  2.59 us

profile of v3, /device:TPU:0, one launch (start us, length us, event | category | flops | bytes accessed | tf_op | source)
XLA Modules:
  0.0 57.6 jit_solution(16169620802488941828)
XLA Ops:
  0.6 50.2 %shard_map.67 = (bf16[4096,256]{1,0:T(8,128)(2,1)}, bf16[4096,256]{1,0:T(8,128)(2,1)}, f32[12,64,64]{2,1,0:T(8,128)}) custom-call(bf16[4096,256]{1,0:T(8,128)(2,1)} %bitcast.7, bf16[768,256]{1,0:T(8,128)(2,1)} %bitcast.10, bf16[2304,256]{1,0:T(8,128)(2,1)} %bitcast.9, bf16[4096,256]{1,0:T(8,128)(2,1)} %bitcast.8), custom_call_target="tpu_custom_call" | custom-call | tf_op jit(solution)/shard_map/pallas_call | solution.py:399
  50.9 0.0 copy-start
  50.9 1.6 %copy-done = bf16[4096,256]{1,0:T(8,128)(2,1)S(1)} copy-done((bf16[4096,256]{1,0:T(8,128)(2,1)S(1)}, bf16[4096,256]{1,0:T(8,128)(2,1)}, u32[]{:S(2)}) %copy-start) | copy-done | bytes 2097176
  52.4 0.0 copy-start.1
  52.4 1.6 %copy-done.1 = bf16[4096,256]{1,0:T(8,128)(2,1)S(1)} copy-done((bf16[4096,256]{1,0:T(8,128)(2,1)S(1)}, bf16[4096,256]{1,0:T(8,128)(2,1)}, u32[]{:S(2)}) %copy-start.1) | copy-done | bytes 2097176
  54.0 0.0 copy-start.2
  54.0 1.0 %copy-done.2 = f32[12,64,64]{2,1,0:T(8,128)S(1)} copy-done((f32[12,64,64]{2,1,0:T(8,128)S(1)}, f32[12,64,64]{2,1,0:T(8,128)}, u32[]{:S(2)}) %copy-start.2) | copy-done | bytes 196632
  55.0 2.6 %shard_map.68 = (bf16[4096,256]{1,0:T(8,128)(2,1)}, bf16[4096,256]{1,0:T(8,128)(2,1)}, f32[12,64,64]{2,1,0:T(8,128)}) custom-call(bf16[4096,256]{1,0:T(8,128)(2,1)S(1)} %copy-done, bf16[4096,256]{1,0:T(8,128)(2,1)S(1)} %copy-done.1, f32[12,64,64]{2,1,0:T(8,128)S(1)} %copy-done.2), custom_call_target="tpu_custom_call" | custom-call | bytes 8388608 | tf_op jit(solution)/shard_map/pallas_call | solution.py:421
Async XLA Ops:
  50.9 1.6 %copy-start = (bf16[4096,256]{1,0:T(8,128)(2,1)S(1)}, bf16[4096,256]{1,0:T(8,128)(2,1)}, u32[]{:S(2)}) copy-start(bf16[4096,256]{1,0:T(8,128)(2,1)} %get-tuple-element.9.refs_0_) | copy-start | bytes 6291460
  52.4 1.6 %copy-start.1 = (bf16[4096,256]{1,0:T(8,128)(2,1)S(1)}, bf16[4096,256]{1,0:T(8,128)(2,1)}, u32[]{:S(2)}) copy-start(bf16[4096,256]{1,0:T(8,128)(2,1)} %get-tuple-element.10.refs_1_) | copy-start | bytes 6291460
  54.0 1.0 %copy-start.2 = (f32[12,64,64]{2,1,0:T(8,128)S(1)}, f32[12,64,64]{2,1,0:T(8,128)}, u32[]{:S(2)}) copy-start(f32[12,64,64]{2,1,0:T(8,128)} %get-tuple-element.11.refs_2_) | copy-start | bytes 589828

commit v4 on v3

--- a/solution.py
+++ b/solution.py
@@ -428,7 +428,7 @@
         ),
         in_specs=[tile, tile, full],
         out_specs=(tile, tile, full),
-        compiler_params=pltpu.CompilerParams(vmem_limit_bytes=24 * 2**20),
+        compiler_params=pltpu.CompilerParams(vmem_limit_bytes=60 * 2**20),
         cost_estimate=pl.CostEstimate(flops=0, bytes_accessed=8 * rows * ch, transcendentals=0),
     )(output, grad_input, grads)
     grads = jnp.transpose(grads, (1, 0, 2))

time: 57.8 us -> 56 us (0.969)
  local copies, waits for them, and re-layouts: 4.17 us -> 0 us
  Pallas kernels: 52.8 us -> 55.1 us
    unnamed x6 -> x0, local copies, waits for them, and re-layouts: 4.17 us -> none
    pallas_call x1, Pallas kernels: 2.59 us -> 4.94 us  [local(): pl.pallas_call(hand_on, grid=(steps,), out_shape=(shape((rows, ch), BF16)...]
where the time goes in v4:
time: 56 us; the launch traced here: 55.8 us
  Pallas kernels  55.1 us (98%)
  between operations  0.64 us (1%)
    pallas_call x1, Pallas kernels, local(): pl.pallas_call(functools.partial(kernel, cfg), out_shape=(shape((rows, ch...  50.2 us
    pallas_call x1, Pallas kernels, local(): pl.pallas_call(hand_on, grid=(steps,), out_shape=(shape((rows, ch), BF16)...  4.94 us

profile of v4, /device:TPU:0, one launch (start us, length us, event | category | flops | bytes accessed | tf_op | source)
XLA Modules:
  0.0 55.8 jit_solution(13170466758496142982)
XLA Ops:
  0.6 50.2 %shard_map.67 = (bf16[4096,256]{1,0:T(8,128)(2,1)}, bf16[4096,256]{1,0:T(8,128)(2,1)}, f32[12,64,64]{2,1,0:T(8,128)}) custom-call(bf16[4096,256]{1,0:T(8,128)(2,1)} %bitcast.7, bf16[768,256]{1,0:T(8,128)(2,1)} %bitcast.10, bf16[2304,256]{1,0:T(8,128)(2,1)} %bitcast.9, bf16[4096,256]{1,0:T(8,128)(2,1)} %bitcast.8), custom_call_target="tpu_custom_call" | custom-call | tf_op jit(solution)/shard_map/pallas_call | solution.py:399
  50.8 4.9 %shard_map.68 = (bf16[4096,256]{1,0:T(8,128)(2,1)}, bf16[4096,256]{1,0:T(8,128)(2,1)}, f32[12,64,64]{2,1,0:T(8,128)}) custom-call(bf16[4096,256]{1,0:T(8,128)(2,1)} %get-tuple-element.9.refs_0_, bf16[4096,256]{1,0:T(8,128)(2,1)} %get-tuple-element.10.refs_1_, f32[12,64,64]{2,1,0:T(8,128)} %get-tuple-element.11.refs_2_), custom_call_target="tpu_custom_call" | custom-call | bytes 8388608 | tf_op jit(solution)/shard_map/pallas_call | solution.py:421
